TPU v7x, 32 devices: a whole 2x2x4 slice. The times are simulated.
32 devices in a mesh: dp: 16 (over z, x, core), pipe: 2 (over y).
Axes of the slice: x: 2, y: 2, z: 4, core: 2. Of those that a mesh axis runs over, the one named last changes fastest.
Arguments:
- acts: bfloat16 [2, 2, 1024, 4224], P('pipe', None, 'dp'), may hold values from -6 to 6
- out_grad: bfloat16 [2, 1024, 4224], P(None, 'dp'), may hold values from -6 to 6
- params: bfloat16 [2, 768, 4224], P('pipe'), may hold values from -0.09375 to 0.09375
- moment: float32 [2, 1081344], P('pipe', 'dp'), may hold values from -2 to 2
- second: float32 [2, 1081344], P('pipe', 'dp'), may hold values from 0.0001 to 0.01
Outputs:
- in_grad: bfloat16 [2, 2, 1024, 4224], P('pipe', None, 'dp')
- new_moment: float32 [2, 1081344], P('pipe', 'dp')
- new_second: float32 [2, 1081344], P('pipe', 'dp')
- update: float32 [2, 1081344], P('pipe', 'dp')
All inputs are finite; a program needn't handle non-finite values.
Results may differ from a plain program's by a relative error of at most 0.0056.
Values may be sent and summed in bfloat16 or wider, within the bound.
A program may use at most 64 MiB of HBM per device.

v0:
```python
import jax
import jax.numpy as jnp
from jax import lax
from jax.sharding import PartitionSpec as P


def from_behind(value, axis, steps):
    count = lax.axis_size(axis)
    leading, last = (max(0, -steps), min(count, count - steps))
    return lax.ppermute(value, axis, [(source, source + steps) for source in range(leading, last)])


def backward(inputs, grad_rows, weights_in, weights_down):
    block_size = weights_down.shape[0]
    gate_up = lax.dot_general(
        inputs, weights_in, (((1,), (1,)), ((), ())), preferred_element_type=jnp.float32
    )
    gate_values = gate_up[:, :block_size]
    up_values = gate_up[:, block_size:]
    sigmoid_gate = jax.nn.sigmoid(gate_values)
    activated = gate_values * sigmoid_gate
    d_hidden = lax.dot_general(
        grad_rows, weights_down, (((1,), (1,)), ((), ())), preferred_element_type=jnp.float32
    )
    d_gate = d_hidden * up_values * sigmoid_gate * (1.0 + gate_values * (1.0 - sigmoid_gate))
    d_up = d_hidden * activated
    d_gate_up = jnp.concatenate([d_gate, d_up], axis=1).astype(jnp.bfloat16)
    hidden = (activated * up_values).astype(jnp.bfloat16)
    passed = grad_rows.astype(jnp.float32) + jnp.dot(
        d_gate_up, weights_in, preferred_element_type=jnp.float32
    )
    return (passed.astype(jnp.bfloat16), hidden)


def place_slot(stack, value, slot_index, active):
    previous = lax.dynamic_index_in_dim(stack, slot_index, 0, keepdims=False)
    return lax.dynamic_update_index_in_dim(stack, jnp.where(active, value, previous), slot_index, 0)


def weight_terms(hidden, grad_rows):
    lower = lax.dot_general(
        hidden, grad_rows, (((0,), (0,)), ((), ())), preferred_element_type=jnp.float32
    )
    return lower.reshape(-1)


def local(acts, out_grad, params, moment, second):
    sections = lax.axis_size("pipe")
    section_index = lax.axis_index("pipe")
    inputs = acts[0]
    micro_count = inputs.shape[0]
    tok_rows = inputs.shape[1]
    weights = params[0]
    block_size = weights.shape[0] // 3
    weights_in = weights[: 2 * block_size]
    weights_down = weights[2 * block_size :]
    in_grads = jnp.zeros_like(inputs)
    arrived = jnp.zeros_like(inputs)
    hiddens = jnp.zeros((micro_count, tok_rows, block_size), jnp.bfloat16)
    incoming = jnp.zeros_like(inputs[0])
    tick_count = sections + micro_count - 1
    for tick_index in range(tick_count):
        offset = tick_index - (sections - 1) + section_index
        active = jnp.logical_and(offset >= 0, offset < micro_count)
        slot_index = jnp.clip(offset, 0, micro_count - 1)
        current = lax.dynamic_index_in_dim(inputs, slot_index, 0, keepdims=False)
        top_grad = lax.dynamic_index_in_dim(out_grad, slot_index, 0, keepdims=False)
        grad_rows = jnp.where(section_index == sections - 1, top_grad, incoming)

        def working(current=current, grad_rows=grad_rows):
            return backward(current, grad_rows, weights_in, weights_down)

        def resting(current=current):
            return (jnp.zeros_like(current), jnp.zeros((tok_rows, block_size), jnp.bfloat16))

        passed, hidden = lax.cond(active, working, resting)
        in_grads = place_slot(in_grads, passed, slot_index, active)
        arrived = place_slot(arrived, grad_rows, slot_index, active)
        hiddens = place_slot(hiddens, hidden, slot_index, active)
        if tick_index + 1 < tick_count:
            incoming = from_behind(passed, "pipe", -1)
    row_count = micro_count * tok_rows
    pieces = []
    for micro_index in range(micro_count):
        term = weight_terms(hiddens[micro_index], arrived[micro_index])
        pieces.append(lax.psum_scatter(term, "dp", scatter_dimension=0, tiled=True))
    summed = pieces[0]
    for piece in pieces[1:]:
        summed = summed + piece
    grad_scale = float(row_count * lax.axis_size("dp")) ** (-0.5)
    gradient = summed * grad_scale
    new_moment = 0.9 * moment[0] + 0.1 * gradient
    new_second = 0.999 * second[0] + 0.001 * gradient * gradient
    update = new_moment / (1.0 - 0.9**10) / (jnp.sqrt(new_second / (1.0 - 0.999**10)) + 1e-08)
    return (in_grads[None], new_moment[None], new_second[None], update[None])


def solution(mesh):
    placed = (
        P("pipe", None, "dp", None),
        P(None, "dp", None),
        P("pipe", None, None),
        P("pipe", "dp"),
        P("pipe", "dp"),
    )
    return jax.shard_map(
        local,
        mesh=mesh,
        in_specs=placed,
        out_specs=(P("pipe", None, "dp", None), P("pipe", "dp"), P("pipe", "dp"), P("pipe", "dp")),
        check_vma=False,
    )
```

profile of v0, /device:TPU:0, one launch (start us, length us, event | category | flops | bytes accessed | tf_op | source)
XLA Modules:
  0.0 196.8 jit_solution(378892801083097026)
XLA Ops:
  7.2 0.0 all-reduce.3.cloned.1.call-start
  7.2 1.8 slice_bitcast_fusion.1
  9.0 4.5 %slice_bitcast_fusion = bf16[512,4224]{1,0:T(8,128)(2,1)} fusion(bf16[1,768,4224]{2,1,0:T(8,128)(2,1)} %param.13), kind=kLoop, calls=%fused_computation.48 | loop fusion | bytes 8650752 | tf_op jit(solution)/shard_map/slice | solution.py:55
  13.5 0.1 broadcast.56.clone
  13.6 0.0 copy-start.2
  13.6 1.3 select_dynamic-update-slice_fusion
  14.9 0.1 select_n.105
  15.0 0.9 conditional.3
  15.1 0.9 broadcast.44
  16.0 1.3 collective-permute-start
  17.3 1.1 broadcast.56
  18.3 0.9 bitcast_dynamic-update-slice_fusion.4
  19.2 1.2 broadcast_multiply_fusion
  20.4 1.9 broadcast_multiply_fusion.1
  22.4 0.0 copy-start.12
  22.4 0.6 copy-done.12
  23.0 0.7 dynamic-slice.12
  24.4 2.1 %constant_dynamic-slice_fusion.1 = (bf16[1,64,4224]{2,1,0:T(8,128)(2,1)S(1)}, bf16[1,64,4224]{2,1,0:T(8,128)(2,1)}) fusion(bf16[2,64,4224]{2,1,0:T(8,128)(2,1)S(1)} %get-tuple-element.128, s32[]{:T(128)} %min.11, bf16[2,64,4224]{2,1,0:T(8,128)(2,1)} %bitcast_dynamic-update-slice_fusion.4), kind=kLoop, calls=%fused_computation.78 | loop fusion | bytes 2162692 | tf_op jit(solution)/shard_map/jit(dynamic_index_in_dim)/dynamic_slice | solution.py:36
  26.5 11.8 %collective-permute-done = bf16[64,4224]{1,0:T(8,128)(2,1)} collective-permute-done((bf16[64,4224]{1,0:T(8,128)(2,1)}, bf16[64,4224]{1,0:T(8,128)(2,1)}, u32[]{:S(2)}, u32[]{:S(2)}) %collective-permute-start) | collective-permute-done | bytes 540704 | tf_op jit(solution)/shard_map/ppermute | solution.py:10
  38.3 1.4 bitcast_dynamic-update-slice_fusion.1
  39.8 4.2 %conditional.4 = (bf16[64,4224]{1,0:T(8,128)(2,1)S(1)}, bf16[64,256]{1,0:T(8,128)(2,1)S(1)}) conditional(s32[]{:T(128)} %convert_element_type.52, () %tuple.40, (bf16[64,4224]{1,0:T(8,128)(2,1)S(1)}, bf16[256,4224]{1,0:T(8,128)(2,1)S(1)}, bf16[1,2,64,4224]{3,2,1,0:T(8,128)(2,1)}, s32[]{:T(128)}, bf16[512,4224]{1,0:T(8,128)(2,1)S(1)}) %tuple.65), branch_computations={%region_2.3_spmd, %region_3.4_spmd} | conditional | flops 693248000 | bytes 13402640 | solution.py:76
  39.8 2.5 %fusion.12 = f32[64,512]{1,0:T(8,128)S(1)} fusion(bf16[512,4224]{1,0:T(8,128)(2,1)S(1)} %get-tuple-element.90, bf16[1,2,64,4224]{3,2,1,0:T(8,128)(2,1)} %get-tuple-element.88, s32[]{:T(128)} %get-tuple-element.89), kind=kOutput, calls=%fused_computation.19 | convolution fusion | flops 276824064 | bytes 4997632 | tf_op jit(solution)/shard_map/cond/branch_1_fun/dot_general | solution.py:15
  42.2 0.8 multiply_convert_fusion.5
  43.0 0.9 fusion.11
  44.0 0.0 copy-start.4
  44.0 1.4 collective-permute-start.1
  45.4 0.6 bitcast_dynamic-update-slice_fusion.6
  46.0 0.8 constant_dynamic-slice_fusion.2
  46.8 0.0 copy-start.3
  46.8 12.6 %collective-permute-done.1 = bf16[64,4224]{1,0:T(8,128)(2,1)S(1)} collective-permute-done((bf16[64,4224]{1,0:T(8,128)(2,1)S(1)}, bf16[64,4224]{1,0:T(8,128)(2,1)S(1)}, u32[]{:S(2)}, u32[]{:S(2)}) %collective-permute-start.1) | collective-permute-done | bytes 540704 | tf_op jit(solution)/shard_map/ppermute | solution.py:10
  59.5 0.3 bitcast_dynamic-update-slice_fusion
  59.7 5.5 %conditional.5 = (bf16[64,4224]{1,0:T(8,128)(2,1)S(1)}, bf16[64,256]{1,0:T(8,128)(2,1)S(1)}) conditional(s32[]{:T(128)} %convert_element_type.53, () %tuple.42, (bf16[64,4224]{1,0:T(8,128)(2,1)S(1)}, bf16[256,4224]{1,0:T(8,128)(2,1)S(1)}, bf16[1,2,64,4224]{3,2,1,0:T(8,128)(2,1)S(1)}, s32[]{:T(128)}, bf16[512,4224]{1,0:T(8,128)(2,1)}) %tuple.67), branch_computations={%region_4.5_spmd, %region_5.6_spmd} | conditional | flops 693248000 | bytes 30703664 | solution.py:76
  59.8 3.8 %fusion.22 = f32[64,512]{1,0:T(8,128)S(1)} fusion(bf16[512,4224]{1,0:T(8,128)(2,1)} %get-tuple-element.95, bf16[1,2,64,4224]{3,2,1,0:T(8,128)(2,1)S(1)} %get-tuple-element.93, s32[]{:T(128)} %get-tuple-element.94), kind=kOutput, calls=%fused_computation.34 | convolution fusion | flops 276824064 | bytes 4997124 | tf_op jit(solution)/shard_map/cond/branch_1_fun/dot_general | solution.py:15
  63.6 0.8 multiply_convert_fusion.8
  64.4 0.9 fusion.21
  65.3 0.7 bitcast_dynamic-update-slice_fusion.5
  66.0 1.6 fusion.31
  67.6 2.8 %convolution_add_fusion.3 = f32[256,4224]{1,0:T(8,128)} fusion(f32[256,4224]{1,0:T(8,128)S(1)} %fusion.31, bf16[2,64,4224]{2,1,0:T(8,128)(2,1)S(1)} %get-tuple-element.115, bf16[2,64,256]{2,1,0:T(8,128)(2,1)S(1)} %copy-done.13), kind=kOutput, calls=%fused_computation.47 | convolution fusion | flops 139493376 | bytes 9224192 | tf_op jit(solution)/shard_map/dot_general | solution.py:41
  70.4 4.9 %reshape.31 = f32[1081344]{0:T(1024)} reshape(f32[256,4224]{1,0:T(8,128)} %convolution_add_fusion.3) | data formatting | bytes 8650752 | tf_op jit(solution)/shard_map/add | solution.py:89
  75.3 0.0 all-reduce.3.cloned.1.call-update
  75.3 1.0 copy-done.6
  76.3 0.2 copy-done.9
  76.5 0.9 bitcast_dynamic-update-slice_fusion.3
  77.4 1.3 copy.26
  78.7 0.1 copy-done.8
  78.8 1.2 bitcast_dynamic-update-slice_fusion.2
  80.0 108.0 %all-reduce.3.cloned.1.call-done = f32[1081344]{0:T(1024)} async-done(((f32[1081344]{0:T(1024)}), f32[1081344]{0:T(1024)}) %all-reduce.3.cloned.1.call-update) | async-done | bytes 4325392
  188.1 1.9 add_divide_fusion.3
  (28 shorter events, 0.1 us)
Async XLA Ops:
  7.2 180.9 %all-reduce.3.cloned.1.call-start = ((), (), s32[]{:S(2)}) async-start(), calls=%async_computation | async-start | bytes 8650752
  13.6 1.4 copy-start.2
  16.0 22.3 %collective-permute-start = (bf16[64,4224]{1,0:T(8,128)(2,1)}, bf16[64,4224]{1,0:T(8,128)(2,1)}, u32[]{:S(2)}, u32[]{:S(2)}) collective-permute-start(bf16[64,4224]{1,0:T(8,128)(2,1)} %get-tuple-element.106), channel_id=1, source_target_pairs={{1,0},{3,2},{5,4},{7,6},{9,8},{11,10},{13,12},{15,14},{17,16},{19,... | collective-permute-start | bytes 1622024 | tf_op jit(solution)/shard_map/ppermute | solution.py:10
  18.3 4.7 %copy-start.14 = (u32[32]{0:T(128)S(1)}, u32[32]{0:T(128)}, u32[]{:S(2)}) copy-start(u32[32]{0:T(128)} %constant.132) | copy-start | bytes 388
  22.4 0.6 copy-start.12
  24.4 15.4 %copy-start = (bf16[512,4224]{1,0:T(8,128)(2,1)S(1)}, bf16[512,4224]{1,0:T(8,128)(2,1)}, u32[]{:S(2)}) copy-start(bf16[512,4224]{1,0:T(8,128)(2,1)} %slice_bitcast_fusion) | copy-start | bytes 12976132
  44.0 15.8 %copy-start.5 = (bf16[64,4224]{1,0:T(8,128)(2,1)}, bf16[64,4224]{1,0:T(8,128)(2,1)S(1)}, u32[]{:S(2)}) copy-start(bf16[64,4224]{1,0:T(8,128)(2,1)S(1)} %get-tuple-element.107) | copy-start | bytes 1622020
  44.0 15.5 %copy-start.4 = (bf16[2,64,4224]{2,1,0:T(8,128)(2,1)S(1)}, bf16[2,64,4224]{2,1,0:T(8,128)(2,1)}, u32[]{:S(2)}) copy-start(bf16[2,64,4224]{2,1,0:T(8,128)(2,1)} %param.12) | copy-start | bytes 3244036
  44.0 15.5 %collective-permute-start.1 = (bf16[64,4224]{1,0:T(8,128)(2,1)S(1)}, bf16[64,4224]{1,0:T(8,128)(2,1)S(1)}, u32[]{:S(2)}, u32[]{:S(2)}) collective-permute-start(bf16[64,4224]{1,0:T(8,128)(2,1)S(1)} %get-tuple-element.107), channel_id=1, source_target_pairs={{1,0},{3,2},{5,4},{7,6},{9,8},{11,10},{13,12},{15,14},{17,16},{19,... | collective-permute-start | bytes 1622024 | tf_op jit(solution)/shard_map/ppermute | solution.py:10
  46.8 12.9 %copy-start.3 = (bf16[1,2,64,4224]{3,2,1,0:T(8,128)(2,1)S(1)}, bf16[1,2,64,4224]{3,2,1,0:T(8,128)(2,1)}, u32[]{:S(2)}) copy-start(bf16[1,2,64,4224]{3,2,1,0:T(8,128)(2,1)} %param.11) | copy-start | bytes 3244036
  59.8 4.6 %copy-start.1 = (bf16[512,4224]{1,0:T(8,128)(2,1)S(1)}, bf16[512,4224]{1,0:T(8,128)(2,1)}, u32[]{:S(2)}) copy-start(bf16[512,4224]{1,0:T(8,128)(2,1)} %get-tuple-element.95) | copy-start | bytes 12976132 | tf_op jit(solution)/shard_map/cond
  65.3 2.3 %copy-start.7 = (bf16[64,4224]{1,0:T(8,128)(2,1)}, bf16[64,4224]{1,0:T(8,128)(2,1)S(1)}, u32[]{:S(2)}) copy-start(bf16[64,4224]{1,0:T(8,128)(2,1)S(1)} %get-tuple-element.108) | copy-start | bytes 1622020
  66.0 1.6 copy-start.13
  75.3 1.0 copy-start.6
  75.3 1.2 copy-start.9
  77.4 1.4 copy-start.8
  78.7 109.4 %copy-start.11 = (f32[1,67584]{1,0:T(1,128)S(1)}, f32[1,67584]{1,0:T(1,128)}, u32[]{:S(2)}) copy-start(f32[1,67584]{1,0:T(1,128)} %broadcast_multiply_fusion.1) | copy-start | bytes 811012
  80.0 110.0 %copy-start.10 = (bf16[1,2,64,4224]{3,2,1,0:T(8,128)(2,1)}, bf16[1,2,64,4224]{3,2,1,0:T(8,128)(2,1)S(1)}, u32[]{:S(2)}) copy-start(bf16[1,2,64,4224]{3,2,1,0:T(8,128)(2,1)S(1)} %bitcast_dynamic-update-slice_fusion.2) | copy-start | bytes 3244036
Sparse Core Ops, SparseCore 0:
  75.4 112.5 all-reduce.2
where the time goes:
time: 198 us; the launch traced here: 197 us
  waiting for transfers between devices  132 us (67%)
  local copies, waits for them, and re-layouts  20.1 us (10%)
  between operations  14.9 us (8%)
  matrix products  14 us (7%)
  other arithmetic  12.5 us (6%)
  starting transfers between devices  2.74 us (1%)
    unnamed x2, waiting for transfers between devices  108 us
    ppermute x2, waiting for transfers between devices, from_behind(): lax.ppermute(value, axis, [(source, source + steps) for source in range(l...  24.4 us
    dynamic_update_slice x9, other arithmetic, place_slot(): lax.dynamic_update_index_in_dim(stack, jnp.where(active, value, previous)...  7.37 us
    dot_general x2, matrix products, backward(): lax.dot_general(inputs, weights_in, (((1,), (1,)), ((), ())), preferred_e...  6.27 us
    add x1, local copies, waits for them, and re-layouts, local(): summed = summed + piece  4.9 us
    slice x1, local copies, waits for them, and re-layouts, local(): weights_in = weights[:2 * block_size]  4.54 us
    dot_general x2, matrix products, weight_terms(): lax.dot_general(hidden, grad_rows, (((0,), (0,)), ((), ())), preferred_el...  4.39 us
  transfers between devices with their start and end apart: 3, of which 3 were waited for; matrix products, arithmetic and copies ran while one was open for 6% of the time, Pallas kernels for 0%

commit v1 on v0

--- a/solution.py
+++ b/solution.py
@@ -1,7 +1,276 @@
+import functools
+
 import jax
 import jax.numpy as jnp
 from jax import lax
+from jax.experimental import pallas as pl
+from jax.experimental.pallas import tpu as pltpu
 from jax.sharding import PartitionSpec as P
+
+MESH = pl.DeviceIdType.MESH
+NT = (((1,), (1,)), ((), ()))
+
+
+def chunk_width(width):
+    return max((w for w in (128, 256, 384, 512) if width % w == 0), default=0)
+
+
+def kernel(dims, x_hbm, g_hbm, w_hbm, m_ref, s_ref, out_hbm, nm_ref, ns_ref, up_ref,
+           x, g, w, ig, gu, dh, hid, dgu, part, r1, send2, own, r2, send3, r3,
+           load_x, load_g, load_w, store, sy, ry, s1, q1, s2, q2, s3, q3):
+    sections, count, cols, chunks, rows, grad_scale = dims
+    depth = count // 4
+    block = hid.shape[0]
+    sec = lax.axis_index("pipe")
+    me = lax.axis_index("dp")
+    core, xx, zz = lax.rem(me, 2), lax.rem(me // 2, 2), me // 4
+    last = sec == sections - 1
+    core_peer = me + 1 - 2 * core
+    x_peer = me + 2 - 4 * xx
+    z_peers = [me + 4 * (lax.rem(zz + j, depth) - zz) for j in range(1, depth)]
+
+    def at(c):
+        return pl.ds(pl.multiple_of(c * cols, cols), cols)
+
+    def loads(c):
+        return (pltpu.make_async_copy(w_hbm.at[:, at(c)], w.at[:, at(c)], load_w.at[c]),
+                pltpu.make_async_copy(x_hbm.at[:, at(c)], x.at[:, at(c)], load_x.at[c]))
+
+    def load_grad(c):
+        return pltpu.make_async_copy(g_hbm.at[:, at(c)], g.at[:, at(c)], load_g.at[c])
+
+    def relay(c):
+        return pltpu.make_async_remote_copy(
+            ig.at[:, at(c)], g.at[:, at(c)], sy.at[c], ry.at[c],
+            device_id={"pipe": lax.max(sec - 1, 0), "dp": me}, device_id_type=MESH)
+
+    def stage1(c):
+        return pltpu.make_async_remote_copy(
+            part.at[1 - core, :, :, :, at(c)], r1.at[:, :, :, at(c)], s1.at[c], q1.at[c],
+            device_id={"pipe": sec, "dp": core_peer}, device_id_type=MESH)
+
+    def stage2(c):
+        return pltpu.make_async_remote_copy(
+            send2.at[:, :, at(c)], r2.at[:, :, at(c)], s2.at[c], q2.at[c],
+            device_id={"pipe": sec, "dp": x_peer}, device_id_type=MESH)
+
+    def stage3(c, j):
+        return pltpu.make_async_remote_copy(
+            send3.at[lax.rem(zz + j + 1, depth), :, at(c)], r3.at[j, :, at(c)], s3.at[j, c], q3.at[j, c],
+            device_id={"pipe": sec, "dp": z_peers[j]}, device_id_type=MESH)
+
+    def result(c):
+        return pltpu.make_async_copy(ig.at[:, at(c)], out_hbm.at[:, at(c)], store.at[c])
+
+    def each(body, low=0, high=chunks):
+        def step(c, carry):
+            body(c)
+            return carry
+        lax.fori_loop(low, high, step, 0)
+
+    barrier = pltpu.get_barrier_semaphore()
+    for peer in [core_peer, x_peer] + z_peers:
+        pl.semaphore_signal(barrier, inc=1, device_id={"pipe": sec, "dp": peer}, device_id_type=MESH)
+
+    @pl.when(sec > 0)
+    def _():
+        pl.semaphore_signal(barrier, inc=1, device_id={"pipe": lax.max(sec - 1, 0), "dp": me}, device_id_type=MESH)
+
+    @pl.when(jnp.logical_not(last))
+    def _():
+        pl.semaphore_signal(barrier, inc=1, device_id={"pipe": lax.min(sec + 1, sections - 1), "dp": me}, device_id_type=MESH)
+
+    def begin(c):
+        for copy in loads(c):
+            copy.start()
+
+        @pl.when(last)
+        def _():
+            load_grad(c).start()
+
+    each(begin)
+    gu[...] = jnp.zeros_like(gu)
+    dh[...] = jnp.zeros_like(dh)
+
+    def add_hidden_grad(c):
+        dh[...] += lax.dot_general(g[:, at(c)], w[2 * block:, at(c)], NT, preferred_element_type=jnp.float32)
+
+    def forward(c):
+        for copy in loads(c):
+            copy.wait()
+        gu[...] += lax.dot_general(x[:, at(c)], w[: 2 * block, at(c)], NT, preferred_element_type=jnp.float32)
+
+        @pl.when(last)
+        def _():
+            load_grad(c).wait()
+            add_hidden_grad(c)
+
+    each(forward)
+    gate, up = gu[:, :block], gu[:, block:]
+    hid[...] = (gate * jax.nn.sigmoid(gate) * up).T.astype(jnp.bfloat16)
+
+    pl.semaphore_wait(barrier, 1 + depth + lax.min(sec, 1) + lax.min(sections - 1 - sec, 1))
+
+    def input_grad():
+        gate_v, up_v, d = gu[:, :block], gu[:, block:], dh[...]
+        sg = jax.nn.sigmoid(gate_v)
+        dgu[:, :block] = (d * up_v * sg * (1.0 + gate_v * (1.0 - sg))).astype(jnp.bfloat16)
+        dgu[:, block:] = (d * gate_v * sg).astype(jnp.bfloat16)
+
+        def one(c):
+            ig[:, at(c)] = (g[:, at(c)].astype(jnp.float32) + jnp.dot(
+                dgu[...], w[: 2 * block, at(c)], preferred_element_type=jnp.float32)).astype(jnp.bfloat16)
+
+            @pl.when(sec > 0)
+            def _():
+                relay(c).start()
+
+            result(c).start()
+
+        each(one)
+
+    @pl.when(last)
+    def _():
+        input_grad()
+
+    def step(t):
+        @pl.when(t < chunks)
+        def _():
+            @pl.when(jnp.logical_not(last))
+            def _():
+                relay(t).wait_recv()
+
+            term = jnp.dot(hid[...], g[:, at(t)], preferred_element_type=jnp.float32)
+            for owner in range(count):
+                part[owner % 2, owner // 2 % 2, owner // 4, :, at(t)] = term[
+                    owner * rows:(owner + 1) * rows].astype(jnp.bfloat16)
+            stage1(t).start()
+
+            @pl.when(jnp.logical_not(last))
+            def _():
+                add_hidden_grad(t)
+
+        @pl.when(jnp.logical_and(t >= 1, t <= chunks))
+        def _():
+            c = t - 1
+            stage1(c).wait_recv()
+            for z in range(depth):
+                send2[z, :, at(c)] = (part[core, 1 - xx, z, :, at(c)].astype(jnp.float32)
+                                      + r1[1 - xx, z, :, at(c)].astype(jnp.float32)).astype(jnp.bfloat16)
+            stage2(c).start()
+            for z in range(depth):
+                own[z, :, at(c)] = (part[core, xx, z, :, at(c)].astype(jnp.float32)
+                                    + r1[xx, z, :, at(c)].astype(jnp.float32))
+
+        @pl.when(jnp.logical_and(t >= 2, t <= chunks + 1))
+        def _():
+            c = t - 2
+            stage2(c).wait_recv()
+            for z in range(depth):
+                total = own[z, :, at(c)] + r2[z, :, at(c)].astype(jnp.float32)
+                own[z, :, at(c)] = total
+                send3[z, :, at(c)] = total.astype(jnp.bfloat16)
+            for j in range(depth - 1):
+                stage3(c, j).start()
+
+        @pl.when(jnp.logical_and(t == chunks, jnp.logical_not(last)))
+        def _():
+            input_grad()
+
+        @pl.when(t >= 3)
+        def _():
+            c = t - 3
+            total = own[zz, :, at(c)]
+            for j in range(depth - 1):
+                stage3(c, j).wait_recv()
+            for j in range(depth - 1):
+                total = total + r3[j, :, at(c)].astype(jnp.float32)
+            grad = total * grad_scale
+            lanes = cols // 128
+            for k in range(lanes):
+                part_g = grad[:, k * 128:(k + 1) * 128]
+                where = pl.ds(c * lanes + k, rows, stride=chunks * lanes)
+                new_m = 0.9 * m_ref[where, :] + 0.1 * part_g
+                new_s = 0.999 * s_ref[where, :] + 0.001 * part_g * part_g
+                nm_ref[where, :] = new_m
+                ns_ref[where, :] = new_s
+                up_ref[where, :] = new_m / (1.0 - 0.9**10) / (jnp.sqrt(new_s / (1.0 - 0.999**10)) + 1e-08)
+
+    each(step, 0, chunks + 3)
+
+    def finish(c):
+        stage1(c).wait_send()
+        stage2(c).wait_send()
+        for j in range(depth - 1):
+            stage3(c, j).wait_send()
+
+        @pl.when(sec > 0)
+        def _():
+            relay(c).wait_send()
+
+        result(c).wait()
+
+    each(finish)
+
+
+def fused(acts, out_grad, params, moment, second):
+    sections, count = lax.axis_size("pipe"), lax.axis_size("dp")
+    _, micro, tok, width = acts.shape
+    tall = params.shape[1]
+    block = tall // 3
+    total_rows = micro * tok
+    cols = chunk_width(width)
+    chunks = width // cols
+    rows = block // count
+    depth = count // 4
+    flat = (rows * width // 128, 128)
+    grad_scale = float(total_rows * count) ** (-0.5)
+    bf, f32 = jnp.bfloat16, jnp.float32
+    dma = pltpu.SemaphoreType.DMA
+    anywhere = pl.BlockSpec(memory_space=pl.ANY)
+    vmem = pl.BlockSpec(memory_space=pltpu.VMEM)
+    in_grad, nm, ns, up = pl.pallas_call(
+        functools.partial(kernel, (sections, count, cols, chunks, rows, grad_scale)),
+        out_shape=[jax.ShapeDtypeStruct((total_rows, width), bf)] + [jax.ShapeDtypeStruct(flat, f32)] * 3,
+        in_specs=[anywhere] * 3 + [vmem] * 2,
+        out_specs=[anywhere] + [vmem] * 3,
+        scratch_shapes=[
+            pltpu.VMEM((total_rows, width), bf),
+            pltpu.VMEM((total_rows, width), bf),
+            pltpu.VMEM((tall, width), bf),
+            pltpu.VMEM((total_rows, width), bf),
+            pltpu.VMEM((total_rows, 2 * block), f32),
+            pltpu.VMEM((total_rows, block), f32),
+            pltpu.VMEM((block, total_rows), bf),
+            pltpu.VMEM((total_rows, 2 * block), bf),
+            pltpu.VMEM((2, 2, depth, rows, width), bf),
+            pltpu.VMEM((2, depth, rows, width), bf),
+            pltpu.VMEM((depth, rows, width), bf),
+            pltpu.VMEM((depth, rows, width), f32),
+            pltpu.VMEM((depth, rows, width), bf),
+            pltpu.VMEM((depth, rows, width), bf),
+            pltpu.VMEM((depth - 1, rows, width), bf),
+            dma((chunks,)), dma((chunks,)), dma((chunks,)), dma((chunks,)),
+            dma((chunks,)), dma((chunks,)),
+            dma((chunks,)), dma((chunks,)),
+            dma((chunks,)), dma((chunks,)),
+            dma((depth - 1, chunks)), dma((depth - 1, chunks)),
+        ],
+        compiler_params=pltpu.CompilerParams(
+            collective_id=0, has_side_effects=True, vmem_limit_bytes=48 * 1024 * 1024),
+        cost_estimate=pl.CostEstimate(
+            flops=12 * total_rows * block * width, bytes_accessed=2 * tall * width + 10 * total_rows * width,
+            transcendentals=total_rows * block),
+    )(acts.reshape(total_rows, width), out_grad.reshape(total_rows, width), params[0],
+      moment.reshape(flat), second.reshape(flat))
+    return (in_grad.reshape(acts.shape), nm.reshape(moment.shape), ns.reshape(moment.shape), up.reshape(moment.shape))
+
+
+def fits(sizes, acts, params):
+    count, block = sizes["dp"], params.shape[1] // 3
+    micro_rows = acts.shape[1] * acts.shape[2] // count
+    return (count % 4 == 0 and count >= 8 and block % (16 * count) == 0 and block % 128 == 0
+            and micro_rows % 128 == 0 and acts.shape[2] // count % 16 == 0 and chunk_width(acts.shape[3]) > 0)
 
 
 def from_behind(value, axis, steps):
@@ -80,13 +349,8 @@
         if tick_index + 1 < tick_count:
             incoming = from_behind(passed, "pipe", -1)
     row_count = micro_count * tok_rows
-    pieces = []
-    for micro_index in range(micro_count):
-        term = weight_terms(hiddens[micro_index], arrived[micro_index])
-        pieces.append(lax.psum_scatter(term, "dp", scatter_dimension=0, tiled=True))
-    summed = pieces[0]
-    for piece in pieces[1:]:
-        summed = summed + piece
+    term = weight_terms(hiddens.reshape(row_count, block_size), arrived.reshape(row_count, -1))
+    summed = lax.psum_scatter(term, "dp", scatter_dimension=0, tiled=True)
     grad_scale = float(row_count * lax.axis_size("dp")) ** (-0.5)
     gradient = summed * grad_scale
     new_moment = 0.9 * moment[0] + 0.1 * gradient
@@ -103,10 +367,11 @@
         P("pipe", "dp"),
         P("pipe", "dp"),
     )
-    return jax.shard_map(
-        local,
-        mesh=mesh,
-        in_specs=placed,
-        out_specs=(P("pipe", None, "dp", None), P("pipe", "dp"), P("pipe", "dp"), P("pipe", "dp")),
-        check_vma=False,
-    )
+    outs = (P("pipe", None, "dp", None), P("pipe", "dp"), P("pipe", "dp"), P("pipe", "dp"))
+
+    def run(acts, out_grad, params, moment, second):
+        body = fused if fits(mesh.shape, acts, params) else local
+        return jax.shard_map(body, mesh=mesh, in_specs=placed, out_specs=outs, check_vma=False)(
+            acts, out_grad, params, moment, second)
+
+    return run

time: 198 us -> 59.6 us (0.30)
  waiting for transfers between devices: 132 us -> 0 us
  Pallas kernels: 0 us -> 51.3 us
  between operations: 14.9 us -> 0.65 us
  matrix products: 14 us -> 0 us
  local copies, waits for them, and re-layouts: 20.1 us -> 7.47 us
  other arithmetic: 12.5 us -> 0 us
  starting transfers between devices: 2.74 us -> 0 us
    unnamed x2 -> x0, waiting for transfers between devices: 108 us -> none
    pallas_call x0 -> x1, Pallas kernels: none -> 51.3 us  [fused(): pl.pallas_call(functools.partial(kernel, (sections, count, cols, chunks,...]
    ppermute x2 -> x0, waiting for transfers between devices: 24.4 us -> none  [from_behind(): lax.ppermute(value, axis, [(source, source + steps) for source in range(l...]
    dot_general x8 -> x0, matrix products: 14 us -> none  [the longest x2 6.27 us: backward(): lax.dot_general(inputs, weights_in, (((1,), (1,)), ((), ())), preferred_e...]
    dynamic_update_slice x9 -> x0, other arithmetic: 7.37 us -> none  [place_slot(): lax.dynamic_update_index_in_dim(stack, jnp.where(active, value, previous)...]
    slice x2 -> x0, local copies, waits for them, and re-layouts: 6.3 us -> none  [the longest x1 4.54 us: local(): weights_in = weights[:2 * block_size]]
    add x1 -> x0, local copies, waits for them, and re-layouts: 4.9 us -> none  [local(): summed = summed + piece]
    unnamed x30 -> x12, local copies, waits for them, and re-layouts: 3.89 us -> 7.47 us
  transfers between devices with their start and end apart: 3 -> 0, of which waited for: 3 -> 0; matrix products, arithmetic and copies ran while one was open for 6% -> 0% of each run, Pallas kernels for 0% -> 0%
where the time goes in v1:
time: 59.6 us; the launch traced here: 59.4 us
  Pallas kernels  51.3 us (86%)
  local copies, waits for them, and re-layouts  7.47 us (13%)
  between operations  0.65 us (1%)
    pallas_call x1, Pallas kernels, fused(): pl.pallas_call(functools.partial(kernel, (sections, count, cols, chunks,...  51.3 us
    unnamed x12, local copies, waits for them, and re-layouts  7.47 us

profile of v1, /device:TPU:0, one launch (start us, length us, event | category | flops | bytes accessed | tf_op | source)
XLA Modules:
  0.0 59.4 jit_solution(276904926506353833)
XLA Ops:
  0.6 0.0 copy-start
  0.6 1.2 %copy-done = bf16[1,2,64,4224]{3,2,1,0:T(8,128)(2,1)S(1)} copy-done((bf16[1,2,64,4224]{3,2,1,0:T(8,128)(2,1)S(1)}, bf16[1,2,64,4224]{3,2,1,0:T(8,128)(2,1)}, u32[]{:S(2)}) %copy-start) | copy-done | bytes 1081368
  1.9 0.0 copy-start.1
  1.9 1.2 %copy-done.1 = bf16[2,64,4224]{2,1,0:T(8,128)(2,1)S(1)} copy-done((bf16[2,64,4224]{2,1,0:T(8,128)(2,1)S(1)}, bf16[2,64,4224]{2,1,0:T(8,128)(2,1)}, u32[]{:S(2)}) %copy-start.1) | copy-done | bytes 1081368
  3.1 0.0 copy-start.2
  3.1 1.0 %copy-done.2 = f32[1,67584]{1,0:T(1,128)S(1)} copy-done((f32[1,67584]{1,0:T(1,128)S(1)}, f32[1,67584]{1,0:T(1,128)}, u32[]{:S(2)}) %copy-start.2) | copy-done | bytes 270360
  4.1 0.0 copy-start.3
  4.1 1.0 %copy-done.3 = f32[1,67584]{1,0:T(1,128)S(1)} copy-done((f32[1,67584]{1,0:T(1,128)S(1)}, f32[1,67584]{1,0:T(1,128)}, u32[]{:S(2)}) %copy-start.3) | copy-done | bytes 270360
  5.0 51.3 %shard_map.84 = (bf16[128,4224]{1,0:T(8,128)(2,1)S(1)}, f32[528,128]{1,0:T(8,128)S(1)}, f32[528,128]{1,0:T(8,128)S(1)}, f32[528,128]{1,0:T(8,128)S(1)}) custom-call(bf16[128,4224]{1,0:T(8,128)(2,1)S(1)} %bitcast.9, bf16[128,4224]{1,0:T(8,128)(2,1)S(1)} %bitcast.10, bf16[768,4224]{1,0:T(8,128)(2,1)} %bitcast.17, f32[528,128]{1,0:T(8,128)S(1)} %bitcast.15, ...), custom_call_target="tpu_custom_call" | custom-call | flops 1660944384 | bytes 11894784 | tf_op jit(solution)/shard_map/pallas_call | solution.py:232
  56.3 1.0 %copy.13 = bf16[1,2,64,4224]{3,2,1,0:T(8,128)(2,1)} copy(bf16[1,2,64,4224]{3,2,1,0:T(8,128)(2,1)S(1)} %bitcast.11) | data formatting | bytes 2162688
  57.3 0.7 %copy.14 = f32[1,67584]{1,0:T(1,128)} copy(f32[1,67584]{1,0:T(1,128)S(1)} %bitcast.14) | data formatting | bytes 540672
  58.0 0.7 %copy.15 = f32[1,67584]{1,0:T(1,128)} copy(f32[1,67584]{1,0:T(1,128)S(1)} %bitcast.13) | data formatting | bytes 540672
  58.7 0.7 %copy.16 = f32[1,67584]{1,0:T(1,128)} copy(f32[1,67584]{1,0:T(1,128)S(1)} %bitcast.12) | data formatting | bytes 540672
Async XLA Ops:
  0.6 1.2 %copy-start = (bf16[1,2,64,4224]{3,2,1,0:T(8,128)(2,1)S(1)}, bf16[1,2,64,4224]{3,2,1,0:T(8,128)(2,1)}, u32[]{:S(2)}) copy-start(bf16[1,2,64,4224]{3,2,1,0:T(8,128)(2,1)} %param.5) | copy-start | bytes 3244036
  1.9 1.2 %copy-start.1 = (bf16[2,64,4224]{2,1,0:T(8,128)(2,1)S(1)}, bf16[2,64,4224]{2,1,0:T(8,128)(2,1)}, u32[]{:S(2)}) copy-start(bf16[2,64,4224]{2,1,0:T(8,128)(2,1)} %param.6) | copy-start | bytes 3244036
  3.1 1.0 %copy-start.2 = (f32[1,67584]{1,0:T(1,128)S(1)}, f32[1,67584]{1,0:T(1,128)}, u32[]{:S(2)}) copy-start(f32[1,67584]{1,0:T(1,128)} %param.8) | copy-start | bytes 811012
  4.1 1.0 %copy-start.3 = (f32[1,67584]{1,0:T(1,128)S(1)}, f32[1,67584]{1,0:T(1,128)}, u32[]{:S(2)}) copy-start(f32[1,67584]{1,0:T(1,128)} %param.9) | copy-start | bytes 811012

commit v2 on v1

--- a/solution.py
+++ b/solution.py
@@ -15,7 +15,7 @@
     return max((w for w in (128, 256, 384, 512) if width % w == 0), default=0)
 
 
-def kernel(dims, x_hbm, g_hbm, w_hbm, m_ref, s_ref, out_hbm, nm_ref, ns_ref, up_ref,
+def kernel(dims, x_hbm, g_hbm, w_hbm, out_hbm, grad_ref,
            x, g, w, ig, gu, dh, hid, dgu, part, r1, send2, own, r2, send3, r3,
            load_x, load_g, load_w, store, sy, ry, s1, q1, s2, q2, s3, q3):
     sections, count, cols, chunks, rows, grad_scale = dims
@@ -33,34 +33,34 @@
         return pl.ds(pl.multiple_of(c * cols, cols), cols)
 
     def loads(c):
-        return (pltpu.make_async_copy(w_hbm.at[:, at(c)], w.at[:, at(c)], load_w.at[c]),
-                pltpu.make_async_copy(x_hbm.at[:, at(c)], x.at[:, at(c)], load_x.at[c]))
+        return (pltpu.make_async_copy(w_hbm.at[:, at(c)], w.at[c], load_w.at[c]),
+                pltpu.make_async_copy(x_hbm.at[:, at(c)], x.at[c], load_x.at[c]))
 
     def load_grad(c):
-        return pltpu.make_async_copy(g_hbm.at[:, at(c)], g.at[:, at(c)], load_g.at[c])
+        return pltpu.make_async_copy(g_hbm.at[:, at(c)], g.at[c], load_g.at[c])
 
     def relay(c):
         return pltpu.make_async_remote_copy(
-            ig.at[:, at(c)], g.at[:, at(c)], sy.at[c], ry.at[c],
+            ig.at[c], g.at[c], sy.at[c], ry.at[c],
             device_id={"pipe": lax.max(sec - 1, 0), "dp": me}, device_id_type=MESH)
 
     def stage1(c):
         return pltpu.make_async_remote_copy(
-            part.at[1 - core, :, :, :, at(c)], r1.at[:, :, :, at(c)], s1.at[c], q1.at[c],
+            part.at[c, 1 - core], r1.at[c], s1.at[c], q1.at[c],
             device_id={"pipe": sec, "dp": core_peer}, device_id_type=MESH)
 
     def stage2(c):
         return pltpu.make_async_remote_copy(
-            send2.at[:, :, at(c)], r2.at[:, :, at(c)], s2.at[c], q2.at[c],
+            send2.at[c], r2.at[c], s2.at[c], q2.at[c],
             device_id={"pipe": sec, "dp": x_peer}, device_id_type=MESH)
 
     def stage3(c, j):
         return pltpu.make_async_remote_copy(
-            send3.at[lax.rem(zz + j + 1, depth), :, at(c)], r3.at[j, :, at(c)], s3.at[j, c], q3.at[j, c],
+            send3.at[c, lax.rem(zz + j + 1, depth)], r3.at[c, j], s3.at[j, c], q3.at[j, c],
             device_id={"pipe": sec, "dp": z_peers[j]}, device_id_type=MESH)
 
     def result(c):
-        return pltpu.make_async_copy(ig.at[:, at(c)], out_hbm.at[:, at(c)], store.at[c])
+        return pltpu.make_async_copy(ig.at[c], out_hbm.at[:, at(c)], store.at[c])
 
     def each(body, low=0, high=chunks):
         def step(c, carry):
@@ -93,12 +93,12 @@
     dh[...] = jnp.zeros_like(dh)
 
     def add_hidden_grad(c):
-        dh[...] += lax.dot_general(g[:, at(c)], w[2 * block:, at(c)], NT, preferred_element_type=jnp.float32)
+        dh[...] += lax.dot_general(g[c], w[c, 2 * block:, :], NT, preferred_element_type=jnp.float32)
 
     def forward(c):
         for copy in loads(c):
             copy.wait()
-        gu[...] += lax.dot_general(x[:, at(c)], w[: 2 * block, at(c)], NT, preferred_element_type=jnp.float32)
+        gu[...] += lax.dot_general(x[c], w[c, : 2 * block, :], NT, preferred_element_type=jnp.float32)
 
         @pl.when(last)
         def _():
@@ -118,8 +118,8 @@
         dgu[:, block:] = (d * gate_v * sg).astype(jnp.bfloat16)
 
         def one(c):
-            ig[:, at(c)] = (g[:, at(c)].astype(jnp.float32) + jnp.dot(
-                dgu[...], w[: 2 * block, at(c)], preferred_element_type=jnp.float32)).astype(jnp.bfloat16)
+            ig[c] = (g[c].astype(jnp.float32) + jnp.dot(
+                dgu[...], w[c, : 2 * block, :], preferred_element_type=jnp.float32)).astype(jnp.bfloat16)
 
             @pl.when(sec > 0)
             def _():
@@ -140,9 +140,9 @@
             def _():
                 relay(t).wait_recv()
 
-            term = jnp.dot(hid[...], g[:, at(t)], preferred_element_type=jnp.float32)
+            term = jnp.dot(hid[...], g[t], preferred_element_type=jnp.float32)
             for owner in range(count):
-                part[owner % 2, owner // 2 % 2, owner // 4, :, at(t)] = term[
+                part[t, owner % 2, owner // 2 % 2, owner // 4] = term[
                     owner * rows:(owner + 1) * rows].astype(jnp.bfloat16)
             stage1(t).start()
 
@@ -155,21 +155,21 @@
             c = t - 1
             stage1(c).wait_recv()
             for z in range(depth):
-                send2[z, :, at(c)] = (part[core, 1 - xx, z, :, at(c)].astype(jnp.float32)
-                                      + r1[1 - xx, z, :, at(c)].astype(jnp.float32)).astype(jnp.bfloat16)
+                send2[c, z] = (part[c, core, 1 - xx, z].astype(jnp.float32)
+                                      + r1[c, 1 - xx, z].astype(jnp.float32)).astype(jnp.bfloat16)
             stage2(c).start()
             for z in range(depth):
-                own[z, :, at(c)] = (part[core, xx, z, :, at(c)].astype(jnp.float32)
-                                    + r1[xx, z, :, at(c)].astype(jnp.float32))
+                own[c, z] = (part[c, core, xx, z].astype(jnp.float32)
+                                    + r1[c, xx, z].astype(jnp.float32))
 
         @pl.when(jnp.logical_and(t >= 2, t <= chunks + 1))
         def _():
             c = t - 2
             stage2(c).wait_recv()
             for z in range(depth):
-                total = own[z, :, at(c)] + r2[z, :, at(c)].astype(jnp.float32)
-                own[z, :, at(c)] = total
-                send3[z, :, at(c)] = total.astype(jnp.bfloat16)
+                total = own[c, z] + r2[c, z].astype(jnp.float32)
+                own[c, z] = total
+                send3[c, z] = total.astype(jnp.bfloat16)
             for j in range(depth - 1):
                 stage3(c, j).start()
 
@@ -180,21 +180,16 @@
         @pl.when(t >= 3)
         def _():
             c = t - 3
-            total = own[zz, :, at(c)]
+            total = own[c, zz]
             for j in range(depth - 1):
                 stage3(c, j).wait_recv()
             for j in range(depth - 1):
-                total = total + r3[j, :, at(c)].astype(jnp.float32)
+                total = total + r3[c, j].astype(jnp.float32)
             grad = total * grad_scale
             lanes = cols // 128
             for k in range(lanes):
-                part_g = grad[:, k * 128:(k + 1) * 128]
                 where = pl.ds(c * lanes + k, rows, stride=chunks * lanes)
-                new_m = 0.9 * m_ref[where, :] + 0.1 * part_g
-                new_s = 0.999 * s_ref[where, :] + 0.001 * part_g * part_g
-                nm_ref[where, :] = new_m
-                ns_ref[where, :] = new_s
-                up_ref[where, :] = new_m / (1.0 - 0.9**10) / (jnp.sqrt(new_s / (1.0 - 0.999**10)) + 1e-08)
+                grad_ref[where, :] = grad[:, k * 128:(k + 1) * 128]
 
     each(step, 0, chunks + 3)
 
@@ -211,6 +206,18 @@
         result(c).wait()
 
     each(finish)
+
+
+def finish_kernel(sent_hbm, grad_ref, m_ref, s_ref, out_hbm, nm_ref, ns_ref, up_ref, sem):
+    copy = pltpu.make_async_copy(sent_hbm, out_hbm, sem)
+    copy.start()
+    grad = grad_ref[...]
+    new_m = 0.9 * m_ref[...] + 0.1 * grad
+    new_s = 0.999 * s_ref[...] + 0.001 * grad * grad
+    nm_ref[...] = new_m
+    ns_ref[...] = new_s
+    up_ref[...] = new_m / (1.0 - 0.9**10) / (jnp.sqrt(new_s / (1.0 - 0.999**10)) + 1e-08)
+    copy.wait()
 
 
 def fused(acts, out_grad, params, moment, second):
@@ -229,27 +236,27 @@
     dma = pltpu.SemaphoreType.DMA
     anywhere = pl.BlockSpec(memory_space=pl.ANY)
     vmem = pl.BlockSpec(memory_space=pltpu.VMEM)
-    in_grad, nm, ns, up = pl.pallas_call(
+    sent, grad = pl.pallas_call(
         functools.partial(kernel, (sections, count, cols, chunks, rows, grad_scale)),
-        out_shape=[jax.ShapeDtypeStruct((total_rows, width), bf)] + [jax.ShapeDtypeStruct(flat, f32)] * 3,
-        in_specs=[anywhere] * 3 + [vmem] * 2,
-        out_specs=[anywhere] + [vmem] * 3,
+        out_shape=[jax.ShapeDtypeStruct((total_rows, width), bf)] + [jax.ShapeDtypeStruct(flat, f32)],
+        in_specs=[anywhere] * 3,
+        out_specs=[anywhere, vmem],
         scratch_shapes=[
-            pltpu.VMEM((total_rows, width), bf),
-            pltpu.VMEM((total_rows, width), bf),
-            pltpu.VMEM((tall, width), bf),
-            pltpu.VMEM((total_rows, width), bf),
+            pltpu.VMEM((chunks, total_rows, cols), bf),
+            pltpu.VMEM((chunks, total_rows, cols), bf),
+            pltpu.VMEM((chunks, tall, cols), bf),
+            pltpu.VMEM((chunks, total_rows, cols), bf),
             pltpu.VMEM((total_rows, 2 * block), f32),
             pltpu.VMEM((total_rows, block), f32),
             pltpu.VMEM((block, total_rows), bf),
             pltpu.VMEM((total_rows, 2 * block), bf),
-            pltpu.VMEM((2, 2, depth, rows, width), bf),
-            pltpu.VMEM((2, depth, rows, width), bf),
-            pltpu.VMEM((depth, rows, width), bf),
-            pltpu.VMEM((depth, rows, width), f32),
-            pltpu.VMEM((depth, rows, width), bf),
-            pltpu.VMEM((depth, rows, width), bf),
-            pltpu.VMEM((depth - 1, rows, width), bf),
+            pltpu.VMEM((chunks, 2, 2, depth, rows, cols), bf),
+            pltpu.VMEM((chunks, 2, depth, rows, cols), bf),
+            pltpu.VMEM((chunks, depth, rows, cols), bf),
+            pltpu.VMEM((chunks, depth, rows, cols), f32),
+            pltpu.VMEM((chunks, depth, rows, cols), bf),
+            pltpu.VMEM((chunks, depth, rows, cols), bf),
+            pltpu.VMEM((chunks, depth - 1, rows, cols), bf),
             dma((chunks,)), dma((chunks,)), dma((chunks,)), dma((chunks,)),
             dma((chunks,)), dma((chunks,)),
             dma((chunks,)), dma((chunks,)),
@@ -257,12 +264,20 @@
             dma((depth - 1, chunks)), dma((depth - 1, chunks)),
         ],
         compiler_params=pltpu.CompilerParams(
-            collective_id=0, has_side_effects=True, vmem_limit_bytes=48 * 1024 * 1024),
+            collective_id=0, has_side_effects=True, vmem_limit_bytes=60 * 1024 * 1024),
         cost_estimate=pl.CostEstimate(
             flops=12 * total_rows * block * width, bytes_accessed=2 * tall * width + 10 * total_rows * width,
             transcendentals=total_rows * block),
-    )(acts.reshape(total_rows, width), out_grad.reshape(total_rows, width), params[0],
-      moment.reshape(flat), second.reshape(flat))
+    )(acts.reshape(total_rows, width), out_grad.reshape(total_rows, width), params[0])
+    in_grad, nm, ns, up = pl.pallas_call(
+        finish_kernel,
+        out_shape=[jax.ShapeDtypeStruct((total_rows, width), bf)] + [jax.ShapeDtypeStruct(flat, f32)] * 3,
+        in_specs=[anywhere] + [vmem] * 3,
+        out_specs=[anywhere] + [vmem] * 3,
+        scratch_shapes=[pltpu.SemaphoreType.DMA],
+        compiler_params=pltpu.CompilerParams(vmem_limit_bytes=60 * 1024 * 1024),
+        cost_estimate=pl.CostEstimate(flops=0, bytes_accessed=4 * total_rows * width, transcendentals=0),
+    )(sent, grad, moment.reshape(flat), second.reshape(flat))
     return (in_grad.reshape(acts.shape), nm.reshape(moment.shape), ns.reshape(moment.shape), up.reshape(moment.shape))
 
 

time: 59.6 us -> 88.4 us (1.48)
  Pallas kernels: 51.3 us -> 87.6 us
  local copies, waits for them, and re-layouts: 7.47 us -> 0 us
    pallas_call x0 -> x1, Pallas kernels: none -> 35.9 us  [fused(): pl.pallas_call(finish_kernel, out_shape=[jax.ShapeDtypeStruct((total_rows...]
    unnamed x12 -> x0, local copies, waits for them, and re-layouts: 7.47 us -> none
where the time goes in v2:
time: 88.4 us; the launch traced here: 88.3 us
  Pallas kernels  87.6 us (99%)
    pallas_call x1, Pallas kernels, fused(): pl.pallas_call(functools.partial(kernel, (sections, count, cols, chunks,...  51.7 us
    pallas_call x1, Pallas kernels, fused(): pl.pallas_call(finish_kernel, out_shape=[jax.ShapeDtypeStruct((total_rows...  35.9 us

profile of v2, /device:TPU:0, one launch (start us, length us, event | category | flops | bytes accessed | tf_op | source)
XLA Modules:
  0.0 88.3 jit_solution(18166262181346509)
XLA Ops:
  0.6 51.7 %shard_map.84 = (bf16[128,4224]{1,0:T(8,128)(2,1)}, f32[528,128]{1,0:T(8,128)}) custom-call(bf16[128,4224]{1,0:T(8,128)(2,1)} %bitcast.10, bf16[128,4224]{1,0:T(8,128)(2,1)} %bitcast.11, bf16[768,4224]{1,0:T(8,128)(2,1)} %bitcast.9), custom_call_target="tpu_custom_call" | custom-call | flops 1660944384 | bytes 11894784 | tf_op jit(solution)/shard_map/pallas_call | solution.py:239
  52.4 35.9 %shard_map.85 = (bf16[128,4224]{1,0:T(8,128)(2,1)}, f32[528,128]{1,0:T(8,128)}, f32[528,128]{1,0:T(8,128)}, f32[528,128]{1,0:T(8,128)}) custom-call(bf16[128,4224]{1,0:T(8,128)(2,1)} %get-tuple-element.10.sent_hbm, f32[528,128]{1,0:T(8,128)} %get-tuple-element.11.grad_ref, f32[528,128]{1,0:T(8,128)} %bitcast.12, f32[528,128]{1,0:T(8,128)} %bitcast.13), custom_call_target="tpu_custom_call" | custom-call | bytes 2162688 | tf_op jit(solution)/shard_map/pallas_call | solution.py:272

commit v3 on v2

--- a/solution.py
+++ b/solution.py
@@ -208,16 +208,19 @@
     each(finish)
 
 
-def finish_kernel(sent_hbm, grad_ref, m_ref, s_ref, out_hbm, nm_ref, ns_ref, up_ref, sem):
-    copy = pltpu.make_async_copy(sent_hbm, out_hbm, sem)
-    copy.start()
+def finish_kernel(sent_ref, grad_ref, m_ref, s_ref, out_hbm, nm_hbm, ns_hbm, up_hbm, nm, ns, up, sem):
+    pairs = ((sent_ref, out_hbm), (nm, nm_hbm), (ns, ns_hbm), (up, up_hbm))
+    copies = [pltpu.make_async_copy(source, target, sem.at[i]) for i, (source, target) in enumerate(pairs)]
+    copies[0].start()
     grad = grad_ref[...]
-    new_m = 0.9 * m_ref[...] + 0.1 * grad
-    new_s = 0.999 * s_ref[...] + 0.001 * grad * grad
-    nm_ref[...] = new_m
-    ns_ref[...] = new_s
-    up_ref[...] = new_m / (1.0 - 0.9**10) / (jnp.sqrt(new_s / (1.0 - 0.999**10)) + 1e-08)
-    copy.wait()
+    nm[...] = 0.9 * m_ref[...] + 0.1 * grad
+    copies[1].start()
+    ns[...] = 0.999 * s_ref[...] + 0.001 * grad * grad
+    copies[2].start()
+    up[...] = nm[...] / (1.0 - 0.9**10) / (jnp.sqrt(ns[...] / (1.0 - 0.999**10)) + 1e-08)
+    copies[3].start()
+    for copy in copies:
+        copy.wait()
 
 
 def fused(acts, out_grad, params, moment, second):
@@ -236,10 +239,11 @@
     dma = pltpu.SemaphoreType.DMA
     anywhere = pl.BlockSpec(memory_space=pl.ANY)
     vmem = pl.BlockSpec(memory_space=pltpu.VMEM)
+    hbm = pl.BlockSpec(memory_space=pltpu.HBM)
     sent, grad = pl.pallas_call(
         functools.partial(kernel, (sections, count, cols, chunks, rows, grad_scale)),
         out_shape=[jax.ShapeDtypeStruct((total_rows, width), bf)] + [jax.ShapeDtypeStruct(flat, f32)],
-        in_specs=[anywhere] * 3,
+        in_specs=[hbm] * 3,
         out_specs=[anywhere, vmem],
         scratch_shapes=[
             pltpu.VMEM((chunks, total_rows, cols), bf),
@@ -264,7 +268,7 @@
             dma((depth - 1, chunks)), dma((depth - 1, chunks)),
         ],
         compiler_params=pltpu.CompilerParams(
-            collective_id=0, has_side_effects=True, vmem_limit_bytes=60 * 1024 * 1024),
+            collective_id=0, has_side_effects=True, vmem_limit_bytes=32 * 1024 * 1024),
         cost_estimate=pl.CostEstimate(
             flops=12 * total_rows * block * width, bytes_accessed=2 * tall * width + 10 * total_rows * width,
             transcendentals=total_rows * block),
@@ -272,10 +276,10 @@
     in_grad, nm, ns, up = pl.pallas_call(
         finish_kernel,
         out_shape=[jax.ShapeDtypeStruct((total_rows, width), bf)] + [jax.ShapeDtypeStruct(flat, f32)] * 3,
-        in_specs=[anywhere] + [vmem] * 3,
-        out_specs=[anywhere] + [vmem] * 3,
-        scratch_shapes=[pltpu.SemaphoreType.DMA],
-        compiler_params=pltpu.CompilerParams(vmem_limit_bytes=60 * 1024 * 1024),
+        in_specs=[vmem] * 4,
+        out_specs=[hbm] * 4,
+        scratch_shapes=[pltpu.VMEM(flat, f32)] * 3 + [dma((4,))],
+        compiler_params=pltpu.CompilerParams(vmem_limit_bytes=16 * 1024 * 1024),
         cost_estimate=pl.CostEstimate(flops=0, bytes_accessed=4 * total_rows * width, transcendentals=0),
     )(sent, grad, moment.reshape(flat), second.reshape(flat))
     return (in_grad.reshape(acts.shape), nm.reshape(moment.shape), ns.reshape(moment.shape), up.reshape(moment.shape))

time: 88.4 us -> 58.5 us (0.66)
  Pallas kernels: 87.6 us -> 52.3 us
  local copies, waits for them, and re-layouts: 0 us -> 5.31 us
    pallas_call x1, Pallas kernels: 35.9 us -> 1.28 us  [fused(): pl.pallas_call(finish_kernel, out_shape=[jax.ShapeDtypeStruct((total_rows...]
    unnamed x0 -> x10, local copies, waits for them, and re-layouts: none -> 5.31 us
where the time goes in v3:
time: 58.5 us; the launch traced here: 58.3 us
  Pallas kernels  52.3 us (89%)
  local copies, waits for them, and re-layouts  5.31 us (9%)
  between operations  0.67 us (1%)
    pallas_call x1, Pallas kernels, fused(): pl.pallas_call(functools.partial(kernel, (sections, count, cols, chunks,...  51 us
    unnamed x10, local copies, waits for them, and re-layouts  5.31 us
    pallas_call x1, Pallas kernels, fused(): pl.pallas_call(finish_kernel, out_shape=[jax.ShapeDtypeStruct((total_rows...  1.28 us

profile of v3, /device:TPU:0, one launch (start us, length us, event | category | flops | bytes accessed | tf_op | source)
XLA Modules:
  0.0 58.3 jit_solution(800903138624593394)
XLA Ops:
  0.6 0.0 copy-start
  0.6 2.8 %copy-done = bf16[1,768,4224]{2,1,0:T(8,128)(2,1)S(1)} copy-done((bf16[1,768,4224]{2,1,0:T(8,128)(2,1)S(1)}, bf16[1,768,4224]{2,1,0:T(8,128)(2,1)}, u32[]{:S(2)}) %copy-start) | copy-done | bytes 6488088
  3.5 0.0 copy-start.1
  3.5 1.2 %copy-done.1 = bf16[1,2,64,4224]{3,2,1,0:T(8,128)(2,1)S(1)} copy-done((bf16[1,2,64,4224]{3,2,1,0:T(8,128)(2,1)S(1)}, bf16[1,2,64,4224]{3,2,1,0:T(8,128)(2,1)}, u32[]{:S(2)}) %copy-start.1) | copy-done | bytes 1081368
  4.7 0.0 copy-start.2
  4.7 1.2 %copy-done.2 = bf16[2,64,4224]{2,1,0:T(8,128)(2,1)S(1)} copy-done((bf16[2,64,4224]{2,1,0:T(8,128)(2,1)S(1)}, bf16[2,64,4224]{2,1,0:T(8,128)(2,1)}, u32[]{:S(2)}) %copy-start.2) | copy-done | bytes 1081368
  5.9 0.0 copy-start.3
  5.9 0.0 copy-start.4
  6.0 51.0 %shard_map.84 = (bf16[128,4224]{1,0:T(8,128)(2,1)S(1)}, f32[528,128]{1,0:T(8,128)S(1)}) custom-call(bf16[128,4224]{1,0:T(8,128)(2,1)S(1)} %bitcast.10, bf16[128,4224]{1,0:T(8,128)(2,1)S(1)} %bitcast.11, bf16[768,4224]{1,0:T(8,128)(2,1)S(1)} %bitcast.9), custom_call_target="tpu_custom_call" | custom-call | flops 1660944384 | bytes 11894784 | tf_op jit(solution)/shard_map/pallas_call | solution.py:243
  57.0 0.0 copy-done.3
  57.0 0.0 copy-done.4
  57.0 1.3 %shard_map.85 = (bf16[128,4224]{1,0:T(8,128)(2,1)}, f32[528,128]{1,0:T(8,128)}, f32[528,128]{1,0:T(8,128)}, f32[528,128]{1,0:T(8,128)}) custom-call(bf16[128,4224]{1,0:T(8,128)(2,1)S(1)} %get-tuple-element.10.sent_ref, f32[528,128]{1,0:T(8,128)S(1)} %get-tuple-element.11.grad_ref, f32[528,128]{1,0:T(8,128)S(1)} %bitcast.12, f32[528,128]{1,0:T(8,128)S(1)} %bitcast.13), custom_call_target="tpu_custom_call" | custom-call | bytes 2162688 | tf_op jit(solution)/shard_map/pallas_call | solution.py:276
Async XLA Ops:
  0.6 2.8 %copy-start = (bf16[1,768,4224]{2,1,0:T(8,128)(2,1)S(1)}, bf16[1,768,4224]{2,1,0:T(8,128)(2,1)}, u32[]{:S(2)}) copy-start(bf16[1,768,4224]{2,1,0:T(8,128)(2,1)} %param.7) | copy-start | bytes 19464196
  3.5 1.2 %copy-start.1 = (bf16[1,2,64,4224]{3,2,1,0:T(8,128)(2,1)S(1)}, bf16[1,2,64,4224]{3,2,1,0:T(8,128)(2,1)}, u32[]{:S(2)}) copy-start(bf16[1,2,64,4224]{3,2,1,0:T(8,128)(2,1)} %param.5) | copy-start | bytes 3244036
  4.7 1.2 %copy-start.2 = (bf16[2,64,4224]{2,1,0:T(8,128)(2,1)S(1)}, bf16[2,64,4224]{2,1,0:T(8,128)(2,1)}, u32[]{:S(2)}) copy-start(bf16[2,64,4224]{2,1,0:T(8,128)(2,1)} %param.6) | copy-start | bytes 3244036
  5.9 51.0 %copy-start.3 = (f32[1,67584]{1,0:T(1,128)S(1)}, f32[1,67584]{1,0:T(1,128)}, u32[]{:S(2)}) copy-start(f32[1,67584]{1,0:T(1,128)} %param.8) | copy-start | bytes 811012
  5.9 51.1 %copy-start.4 = (f32[1,67584]{1,0:T(1,128)S(1)}, f32[1,67584]{1,0:T(1,128)}, u32[]{:S(2)}) copy-start(f32[1,67584]{1,0:T(1,128)} %param.9) | copy-start | bytes 811012

commit v4 on v3

--- a/solution.py
+++ b/solution.py
@@ -268,7 +268,7 @@
             dma((depth - 1, chunks)), dma((depth - 1, chunks)),
         ],
         compiler_params=pltpu.CompilerParams(
-            collective_id=0, has_side_effects=True, vmem_limit_bytes=32 * 1024 * 1024),
+            collective_id=0, has_side_effects=True, vmem_limit_bytes=60 * 1024 * 1024),
         cost_estimate=pl.CostEstimate(
             flops=12 * total_rows * block * width, bytes_accessed=2 * tall * width + 10 * total_rows * width,
             transcendentals=total_rows * block),
@@ -279,7 +279,7 @@
         in_specs=[vmem] * 4,
         out_specs=[hbm] * 4,
         scratch_shapes=[pltpu.VMEM(flat, f32)] * 3 + [dma((4,))],
-        compiler_params=pltpu.CompilerParams(vmem_limit_bytes=16 * 1024 * 1024),
+        compiler_params=pltpu.CompilerParams(vmem_limit_bytes=60 * 1024 * 1024),
         cost_estimate=pl.CostEstimate(flops=0, bytes_accessed=4 * total_rows * width, transcendentals=0),
     )(sent, grad, moment.reshape(flat), second.reshape(flat))
     return (in_grad.reshape(acts.shape), nm.reshape(moment.shape), ns.reshape(moment.shape), up.reshape(moment.shape))

time: 58.5 us -> 55.3 us (0.945)
  local copies, waits for them, and re-layouts: 5.31 us -> 0 us
  Pallas kernels: 52.3 us -> 54.5 us
    unnamed x10 -> x0, local copies, waits for them, and re-layouts: 5.31 us -> none
    pallas_call x1, Pallas kernels: 1.28 us -> 2.72 us  [fused(): pl.pallas_call(finish_kernel, out_shape=[jax.ShapeDtypeStruct((total_rows...]
    pallas_call x1, Pallas kernels: 51 us -> 51.7 us  [fused(): pl.pallas_call(functools.partial(kernel, (sections, count, cols, chunks,...]
where the time goes in v4:
time: 55.3 us; the launch traced here: 55.1 us
  Pallas kernels  54.5 us (99%)
  between operations  0.64 us (1%)
    pallas_call x1, Pallas kernels, fused(): pl.pallas_call(functools.partial(kernel, (sections, count, cols, chunks,...  51.7 us
    pallas_call x1, Pallas kernels, fused(): pl.pallas_call(finish_kernel, out_shape=[jax.ShapeDtypeStruct((total_rows...  2.72 us

profile of v4, /device:TPU:0, one launch (start us, length us, event | category | flops | bytes accessed | tf_op | source)
XLA Modules:
  0.0 55.1 jit_solution(13470820214579339069)
XLA Ops:
  0.6 51.7 %shard_map.84 = (bf16[128,4224]{1,0:T(8,128)(2,1)}, f32[528,128]{1,0:T(8,128)}) custom-call(bf16[128,4224]{1,0:T(8,128)(2,1)} %bitcast.10, bf16[128,4224]{1,0:T(8,128)(2,1)} %bitcast.11, bf16[768,4224]{1,0:T(8,128)(2,1)} %bitcast.9), custom_call_target="tpu_custom_call" | custom-call | flops 1660944384 | bytes 11894784 | tf_op jit(solution)/shard_map/pallas_call | solution.py:243
  52.4 2.7 %shard_map.85 = (bf16[128,4224]{1,0:T(8,128)(2,1)}, f32[528,128]{1,0:T(8,128)}, f32[528,128]{1,0:T(8,128)}, f32[528,128]{1,0:T(8,128)}) custom-call(bf16[128,4224]{1,0:T(8,128)(2,1)} %get-tuple-element.10.sent_ref, f32[528,128]{1,0:T(8,128)} %get-tuple-element.11.grad_ref, f32[528,128]{1,0:T(8,128)} %bitcast.12, f32[528,128]{1,0:T(8,128)} %bitcast.13), custom_call_target="tpu_custom_call" | custom-call | bytes 2162688 | tf_op jit(solution)/shard_map/pallas_call | solution.py:276

commit v5 on v4

--- a/solution.py
+++ b/solution.py
@@ -17,8 +17,9 @@
 
 def kernel(dims, x_hbm, g_hbm, w_hbm, out_hbm, grad_ref,
            x, g, w, ig, gu, dh, hid, dgu, part, r1, send2, own, r2, send3, r3,
-           load_x, load_g, load_w, store, sy, ry, s1, q1, s2, q2, s3, q3):
-    sections, count, cols, chunks, rows, grad_scale = dims
+           load_x, load_g, load_w, store, sy, ry, s1, q1, s2, q2, s3, q3,
+           wa, dgi, sd, qd, sa, qa, sz, qz, sx, qx, sc, qc):
+    sections, count, cols, chunks, rows, grad_scale, helped, first = dims
     depth = count // 4
     block = hid.shape[0]
     sec = lax.axis_index("pipe")
@@ -59,6 +60,40 @@
             send3.at[c, lax.rem(zz + j + 1, depth)], r3.at[c, j], s3.at[j, c], q3.at[j, c],
             device_id={"pipe": sec, "dp": z_peers[j]}, device_id_type=MESH)
 
+    share = 2 * block // count
+    slot = (core * 2 + xx) * depth + zz
+    below = {"pipe": lax.max(sec - 1, 0), "dp": me}
+
+    def order(i):
+        return lax.rem(i + first, chunks)
+
+    def send_share(a):
+        return pltpu.make_async_remote_copy(
+            w.at[first + a, pl.ds(pl.multiple_of(slot * share, share), share)], wa.at[a, core, xx, zz],
+            sa.at[a], qa.at[a], device_id=below, device_id_type=MESH)
+
+    def send_terms():
+        return pltpu.make_async_remote_copy(
+            dgu, dgi, sd.at[0], qd.at[0], device_id=below, device_id_type=MESH)
+
+    def gather_z(a, j):
+        return pltpu.make_async_remote_copy(
+            wa.at[a, core, xx, zz], wa.at[a, core, xx, zz], sz.at[j, a], qz.at[j, a],
+            device_id={"pipe": sec, "dp": z_peers[j]}, device_id_type=MESH)
+
+    def gather_x(a):
+        return pltpu.make_async_remote_copy(
+            wa.at[a, core, xx], wa.at[a, core, xx], sx.at[a], qx.at[a],
+            device_id={"pipe": sec, "dp": x_peer}, device_id_type=MESH)
+
+    def gather_core(a):
+        return pltpu.make_async_remote_copy(
+            wa.at[a, core], wa.at[a, core], sc.at[a], qc.at[a],
+            device_id={"pipe": sec, "dp": core_peer}, device_id_type=MESH)
+
+    def is_helped(c):
+        return jnp.logical_and(c >= first, c < first + helped)
+
     def result(c):
         return pltpu.make_async_copy(ig.at[c], out_hbm.at[:, at(c)], store.at[c])
 
@@ -80,11 +115,12 @@
     def _():
         pl.semaphore_signal(barrier, inc=1, device_id={"pipe": lax.min(sec + 1, sections - 1), "dp": me}, device_id_type=MESH)
 
-    def begin(c):
+    def begin(i):
+        c = order(i)
         for copy in loads(c):
             copy.start()
 
-        @pl.when(last)
+        @pl.when(jnp.logical_or(last, is_helped(c)))
         def _():
             load_grad(c).start()
 
@@ -95,7 +131,8 @@
     def add_hidden_grad(c):
         dh[...] += lax.dot_general(g[c], w[c, 2 * block:, :], NT, preferred_element_type=jnp.float32)
 
-    def forward(c):
+    def forward(i):
+        c = order(i)
         for copy in loads(c):
             copy.wait()
         gu[...] += lax.dot_general(x[c], w[c, : 2 * block, :], NT, preferred_element_type=jnp.float32)
@@ -105,11 +142,25 @@
             load_grad(c).wait()
             add_hidden_grad(c)
 
-    each(forward)
+    each(forward, 0, helped)
+    pl.semaphore_wait(barrier, 1 + depth + lax.min(sec, 1) + lax.min(sections - 1 - sec, 1))
+
+    @pl.when(sec > 0)
+    def _():
+        each(lambda a: send_share(a).start(), 0, helped)
+
+    each(forward, helped, chunks)
     gate, up = gu[:, :block], gu[:, block:]
     hid[...] = (gate * jax.nn.sigmoid(gate) * up).T.astype(jnp.bfloat16)
 
-    pl.semaphore_wait(barrier, 1 + depth + lax.min(sec, 1) + lax.min(sections - 1 - sec, 1))
+    @pl.when(jnp.logical_not(last))
+    def _():
+        def spread(a):
+            send_share(a).wait_recv()
+            for j in range(depth - 1):
+                gather_z(a, j).start()
+
+        each(spread, 0, helped)
 
     def input_grad():
         gate_v, up_v, d = gu[:, :block], gu[:, block:], dh[...]
@@ -117,17 +168,23 @@
         dgu[:, :block] = (d * up_v * sg * (1.0 + gate_v * (1.0 - sg))).astype(jnp.bfloat16)
         dgu[:, block:] = (d * gate_v * sg).astype(jnp.bfloat16)
 
+        @pl.when(sec > 0)
+        def _():
+            send_terms().start()
+
         def one(c):
             ig[c] = (g[c].astype(jnp.float32) + jnp.dot(
                 dgu[...], w[c, : 2 * block, :], preferred_element_type=jnp.float32)).astype(jnp.bfloat16)
 
-            @pl.when(sec > 0)
+            @pl.when(jnp.logical_and(sec > 0, jnp.logical_not(is_helped(c))))
             def _():
                 relay(c).start()
 
             result(c).start()
 
-        each(one)
+        each(one, 0, first)
+        each(one, first + helped, chunks)
+        each(one, first, first + helped)
 
     @pl.when(last)
     def _():
@@ -136,7 +193,36 @@
     def step(t):
         @pl.when(t < chunks)
         def _():
-            @pl.when(jnp.logical_not(last))
+            receives = jnp.logical_not(last)
+
+            @pl.when(jnp.logical_and(receives, t < helped))
+            def _():
+                for j in range(depth - 1):
+                    gather_z(t, j).wait_recv()
+                gather_x(t).start()
+
+            @pl.when(jnp.logical_and(receives, jnp.logical_and(t >= 1, t <= helped)))
+            def _():
+                gather_x(t - 1).wait_recv()
+                gather_core(t - 1).start()
+
+            @pl.when(jnp.logical_and(receives, t == first))
+            def _():
+                send_terms().wait_recv()
+
+            @pl.when(jnp.logical_and(receives, is_helped(t)))
+            def _():
+                a = t - first
+                load_grad(t).wait()
+                gather_core(a).wait_recv()
+                total = g[t].astype(jnp.float32)
+                for k in range(2):
+                    total = total + jnp.dot(
+                        dgi[:, k * block:(k + 1) * block], wa[a, k].reshape(block, cols),
+                        preferred_element_type=jnp.float32)
+                g[t] = total.astype(jnp.bfloat16)
+
+            @pl.when(jnp.logical_and(receives, jnp.logical_not(is_helped(t))))
             def _():
                 relay(t).wait_recv()
 
@@ -199,13 +285,28 @@
         for j in range(depth - 1):
             stage3(c, j).wait_send()
 
-        @pl.when(sec > 0)
+        @pl.when(jnp.logical_and(sec > 0, jnp.logical_not(is_helped(c))))
         def _():
             relay(c).wait_send()
 
         result(c).wait()
 
     each(finish)
+
+    @pl.when(sec > 0)
+    def _():
+        send_terms().wait_send()
+        each(lambda a: send_share(a).wait_send(), 0, helped)
+
+    @pl.when(jnp.logical_not(last))
+    def _():
+        def finish_gather(a):
+            for j in range(depth - 1):
+                gather_z(a, j).wait_send()
+            gather_x(a).wait_send()
+            gather_core(a).wait_send()
+
+        each(finish_gather, 0, helped)
 
 
 def finish_kernel(sent_ref, grad_ref, m_ref, s_ref, out_hbm, nm_hbm, ns_hbm, up_hbm, nm, ns, up, sem):
@@ -233,6 +334,9 @@
     chunks = width // cols
     rows = block // count
     depth = count // 4
+    helped = chunks * 4 // 11
+    first = (chunks - helped + 1) // 2
+    share = 2 * block // count
     flat = (rows * width // 128, 128)
     grad_scale = float(total_rows * count) ** (-0.5)
     bf, f32 = jnp.bfloat16, jnp.float32
@@ -241,7 +345,7 @@
     vmem = pl.BlockSpec(memory_space=pltpu.VMEM)
     hbm = pl.BlockSpec(memory_space=pltpu.HBM)
     sent, grad = pl.pallas_call(
-        functools.partial(kernel, (sections, count, cols, chunks, rows, grad_scale)),
+        functools.partial(kernel, (sections, count, cols, chunks, rows, grad_scale, helped, first)),
         out_shape=[jax.ShapeDtypeStruct((total_rows, width), bf)] + [jax.ShapeDtypeStruct(flat, f32)],
         in_specs=[hbm] * 3,
         out_specs=[anywhere, vmem],
@@ -266,6 +370,13 @@
             dma((chunks,)), dma((chunks,)),
             dma((chunks,)), dma((chunks,)),
             dma((depth - 1, chunks)), dma((depth - 1, chunks)),
+            pltpu.VMEM((helped, 2, 2, depth, share, cols), bf),
+            pltpu.VMEM((total_rows, 2 * block), bf),
+            dma((1,)), dma((1,)),
+            dma((helped,)), dma((helped,)),
+            dma((depth - 1, helped)), dma((depth - 1, helped)),
+            dma((helped,)), dma((helped,)),
+            dma((helped,)), dma((helped,)),
         ],
         compiler_params=pltpu.CompilerParams(
             collective_id=0, has_side_effects=True, vmem_limit_bytes=60 * 1024 * 1024),
@@ -288,7 +399,7 @@
 def fits(sizes, acts, params):
     count, block = sizes["dp"], params.shape[1] // 3
     micro_rows = acts.shape[1] * acts.shape[2] // count
-    return (count % 4 == 0 and count >= 8 and block % (16 * count) == 0 and block % 128 == 0
+    return (sizes["pipe"] == 2 and acts.shape[3] >= 1408 and count % 4 == 0 and count >= 8 and block % (16 * count) == 0 and block % 128 == 0
             and micro_rows % 128 == 0 and acts.shape[2] // count % 16 == 0 and chunk_width(acts.shape[3]) > 0)
 
 

time: 55.3 us -> 61.1 us (1.10)
  Pallas kernels: 54.5 us -> 60.3 us
    pallas_call x1, Pallas kernels: 51.7 us -> 57.6 us  [fused(): pl.pallas_call(functools.partial(kernel, (sections, count, cols, chunks,...]
where the time goes in v5:
time: 61.1 us; the launch traced here: 60.9 us
  Pallas kernels  60.3 us (99%)
  between operations  0.64 us (1%)
    pallas_call x1, Pallas kernels, fused(): pl.pallas_call(functools.partial(kernel, (sections, count, cols, chunks,...  57.6 us
    pallas_call x1, Pallas kernels, fused(): pl.pallas_call(finish_kernel, out_shape=[jax.ShapeDtypeStruct((total_rows...  2.72 us

profile of v5, /device:TPU:0, one launch (start us, length us, event | category | flops | bytes accessed | tf_op | source)
XLA Modules:
  0.0 60.9 jit_solution(8917178960606835009)
XLA Ops:
  0.6 57.6 %shard_map.84 = (bf16[128,4224]{1,0:T(8,128)(2,1)}, f32[528,128]{1,0:T(8,128)}) custom-call(bf16[128,4224]{1,0:T(8,128)(2,1)} %bitcast.10, bf16[128,4224]{1,0:T(8,128)(2,1)} %bitcast.11, bf16[768,4224]{1,0:T(8,128)(2,1)} %bitcast.9), custom_call_target="tpu_custom_call" | custom-call | flops 1660944384 | bytes 11894784 | tf_op jit(solution)/shard_map/pallas_call | solution.py:347
  58.2 2.7 %shard_map.85 = (bf16[128,4224]{1,0:T(8,128)(2,1)}, f32[528,128]{1,0:T(8,128)}, f32[528,128]{1,0:T(8,128)}, f32[528,128]{1,0:T(8,128)}) custom-call(bf16[128,4224]{1,0:T(8,128)(2,1)} %get-tuple-element.10.sent_ref, f32[528,128]{1,0:T(8,128)} %get-tuple-element.11.grad_ref, f32[528,128]{1,0:T(8,128)} %bitcast.12, f32[528,128]{1,0:T(8,128)} %bitcast.13), custom_call_target="tpu_custom_call" | custom-call | bytes 2162688 | tf_op jit(solution)/shard_map/pallas_call | solution.py:387

commit v6 on v4

--- a/solution.py
+++ b/solution.py
@@ -20,6 +20,7 @@
            load_x, load_g, load_w, store, sy, ry, s1, q1, s2, q2, s3, q3):
     sections, count, cols, chunks, rows, grad_scale = dims
     depth = count // 4
+    lag = 2
     block = hid.shape[0]
     sec = lax.axis_index("pipe")
     me = lax.axis_index("dp")
@@ -150,9 +151,9 @@
             def _():
                 add_hidden_grad(t)
 
-        @pl.when(jnp.logical_and(t >= 1, t <= chunks))
-        def _():
-            c = t - 1
+        @pl.when(jnp.logical_and(t >= lag, t < chunks + lag))
+        def _():
+            c = t - lag
             stage1(c).wait_recv()
             for z in range(depth):
                 send2[c, z] = (part[c, core, 1 - xx, z].astype(jnp.float32)
@@ -162,9 +163,9 @@
                 own[c, z] = (part[c, core, xx, z].astype(jnp.float32)
                                     + r1[c, xx, z].astype(jnp.float32))
 
-        @pl.when(jnp.logical_and(t >= 2, t <= chunks + 1))
-        def _():
-            c = t - 2
+        @pl.when(jnp.logical_and(t >= 2 * lag, t < chunks + 2 * lag))
+        def _():
+            c = t - 2 * lag
             stage2(c).wait_recv()
             for z in range(depth):
                 total = own[c, z] + r2[c, z].astype(jnp.float32)
@@ -173,13 +174,13 @@
             for j in range(depth - 1):
                 stage3(c, j).start()
 
-        @pl.when(jnp.logical_and(t == chunks, jnp.logical_not(last)))
+        @pl.when(jnp.logical_and(t == chunks + lag - 1, jnp.logical_not(last)))
         def _():
             input_grad()
 
-        @pl.when(t >= 3)
-        def _():
-            c = t - 3
+        @pl.when(t >= 3 * lag)
+        def _():
+            c = t - 3 * lag
             total = own[c, zz]
             for j in range(depth - 1):
                 stage3(c, j).wait_recv()
@@ -191,7 +192,7 @@
                 where = pl.ds(c * lanes + k, rows, stride=chunks * lanes)
                 grad_ref[where, :] = grad[:, k * 128:(k + 1) * 128]
 
-    each(step, 0, chunks + 3)
+    each(step, 0, chunks + 3 * lag)
 
     def finish(c):
         stage1(c).wait_send()

time: 55.3 us -> 52.5 us (0.949)
  Pallas kernels: 54.5 us -> 51.7 us
    pallas_call x1, Pallas kernels: 51.7 us -> 49 us  [fused(): pl.pallas_call(functools.partial(kernel, (sections, count, cols, chunks,...]
where the time goes in v6:
time: 52.5 us; the launch traced here: 52.4 us
  Pallas kernels  51.7 us (98%)
  between operations  0.64 us (1%)
    pallas_call x1, Pallas kernels, fused(): pl.pallas_call(functools.partial(kernel, (sections, count, cols, chunks,...  49 us
    pallas_call x1, Pallas kernels, fused(): pl.pallas_call(finish_kernel, out_shape=[jax.ShapeDtypeStruct((total_rows...  2.72 us

profile of v6, /device:TPU:0, one launch (start us, length us, event | category | flops | bytes accessed | tf_op | source)
XLA Modules:
  0.0 52.4 jit_solution(1235969695526710723)
XLA Ops:
  0.6 49.0 %shard_map.84 = (bf16[128,4224]{1,0:T(8,128)(2,1)}, f32[528,128]{1,0:T(8,128)}) custom-call(bf16[128,4224]{1,0:T(8,128)(2,1)} %bitcast.10, bf16[128,4224]{1,0:T(8,128)(2,1)} %bitcast.11, bf16[768,4224]{1,0:T(8,128)(2,1)} %bitcast.9), custom_call_target="tpu_custom_call" | custom-call | flops 1660944384 | bytes 11894784 | tf_op jit(solution)/shard_map/pallas_call | solution.py:244
  49.7 2.7 %shard_map.85 = (bf16[128,4224]{1,0:T(8,128)(2,1)}, f32[528,128]{1,0:T(8,128)}, f32[528,128]{1,0:T(8,128)}, f32[528,128]{1,0:T(8,128)}) custom-call(bf16[128,4224]{1,0:T(8,128)(2,1)} %get-tuple-element.10.sent_ref, f32[528,128]{1,0:T(8,128)} %get-tuple-element.11.grad_ref, f32[528,128]{1,0:T(8,128)} %bitcast.12, f32[528,128]{1,0:T(8,128)} %bitcast.13), custom_call_target="tpu_custom_call" | custom-call | bytes 2162688 | tf_op jit(solution)/shard_map/pallas_call | solution.py:277

commit v7 on v6

--- a/solution.py
+++ b/solution.py
@@ -174,7 +174,7 @@
             for j in range(depth - 1):
                 stage3(c, j).start()
 
-        @pl.when(jnp.logical_and(t == chunks + lag - 1, jnp.logical_not(last)))
+        @pl.when(jnp.logical_and(t == chunks + 2 * lag - 1, jnp.logical_not(last)))
         def _():
             input_grad()
 

time: 52.5 us -> 51.5 us (0.981)
  Pallas kernels: 51.7 us -> 50.7 us
    pallas_call x1, Pallas kernels: 49 us -> 48 us  [fused(): pl.pallas_call(functools.partial(kernel, (sections, count, cols, chunks,...]
where the time goes in v7:
time: 51.5 us; the launch traced here: 51.4 us
  Pallas kernels  50.7 us (98%)
  between operations  0.64 us (1%)
    pallas_call x1, Pallas kernels, fused(): pl.pallas_call(functools.partial(kernel, (sections, count, cols, chunks,...  48 us
    pallas_call x1, Pallas kernels, fused(): pl.pallas_call(finish_kernel, out_shape=[jax.ShapeDtypeStruct((total_rows...  2.72 us

profile of v7, /device:TPU:0, one launch (start us, length us, event | category | flops | bytes accessed | tf_op | source)
XLA Modules:
  0.0 51.4 jit_solution(3179879864742607271)
XLA Ops:
  0.6 48.0 %shard_map.84 = (bf16[128,4224]{1,0:T(8,128)(2,1)}, f32[528,128]{1,0:T(8,128)}) custom-call(bf16[128,4224]{1,0:T(8,128)(2,1)} %bitcast.10, bf16[128,4224]{1,0:T(8,128)(2,1)} %bitcast.11, bf16[768,4224]{1,0:T(8,128)(2,1)} %bitcast.9), custom_call_target="tpu_custom_call" | custom-call | flops 1660944384 | bytes 11894784 | tf_op jit(solution)/shard_map/pallas_call | solution.py:244
  48.6 2.7 %shard_map.85 = (bf16[128,4224]{1,0:T(8,128)(2,1)}, f32[528,128]{1,0:T(8,128)}, f32[528,128]{1,0:T(8,128)}, f32[528,128]{1,0:T(8,128)}) custom-call(bf16[128,4224]{1,0:T(8,128)(2,1)} %get-tuple-element.10.sent_ref, f32[528,128]{1,0:T(8,128)} %get-tuple-element.11.grad_ref, f32[528,128]{1,0:T(8,128)} %bitcast.12, f32[528,128]{1,0:T(8,128)} %bitcast.13), custom_call_target="tpu_custom_call" | custom-call | bytes 2162688 | tf_op jit(solution)/shard_map/pallas_call | solution.py:277
